TPU v7x, 32 devices: a whole 2x2x4 slice. The times are simulated.
32 devices in a mesh: groups: 2 (over x), tm: 16 (over z, y, core).
Axes of the slice: x: 2, y: 2, z: 4, core: 2. Of those that a mesh axis runs over, the one named last changes fastest.
Arguments:
- raw: bfloat16 [32768, 3072], P('tm', 'groups'), parts along dimension 1, may hold values from -6 to 6
- taps: float32 [61], replicated, may hold values from -1.5 to 1.5
- whiten: float32 [3072, 33], P('groups'), parts along dimension 0, may hold values from -1.2 to 1.2
- templates: bfloat16 [512, 2048], P('groups'), parts along dimension 0, may hold values from -0.29882812 to 0.29882812
- template_base: int32 [512], P('groups'), parts along dimension 0, may hold values from 0 to 1472, as said below
- amp_scale: float32 [16], P('groups'), parts along dimension 0, may hold values from 0.5 to 2
- spike_time: int32 [32768], P(('groups', 'tm')), parts along dimension 0, may hold values from 0 to 2047, as said below
- spike_template: int32 [32768], P(('groups', 'tm')), parts along dimension 0, may hold values from 0 to 255, as said below
- spike_session: int32 [32768], P(('groups', 'tm')), parts along dimension 0, may hold values from 0 to 7
- live_count: int32 [32], P(('groups', 'tm')), parts along dimension 0, may hold values from 128 to 1024, as said below
Outputs:
- whitened: bfloat16 [32768, 3072], P('tm', 'groups'), parts along dimension 1
- amplitudes: float32 [32768], P(('groups', 'tm')), parts along dimension 0
- new_templates: float32 [512, 2048], P(('groups', 'tm')), parts along dimension 0
There are 2 independent parts, one for each index of `groups`. A program takes and returns all parts, laid end to end along the dimension named above; an argument that names none is the same for every part. Nothing has to cross between parts.
Inputs may be any that keep to these rules, and one draw needn't show every extreme that they name: `template_base`: each template's 64 channels lie within one probe; some template starts at channel 1536 - 64. `live_count`: some time block has all 1024 slots live. `spike_template`: the spike slots of one time block name at most 8 distinct templates among templates j * 16 to j * 16 + 15, for every j; some block names exactly 8 of them for some j. `spike_time`: in every time block one live slot lies at sample 0 and another at sample 2048 - 1.
All inputs are finite; a program needn't handle non-finite values.
Results may differ from a plain program's by a relative error of at most 0.011.
Values may be sent and summed in bfloat16 or wider, within the bound.
A program may use at most 192 MiB of HBM per device.

v0:
```python
import jax
import jax.numpy as jnp
from jax import lax
from jax.sharding import PartitionSpec as P

CH_PROBE = 384
PROBES = 4
BAND = 33
TW = 32
NB = 64
TEMP_DEV = 16


def padded(block, sides, width):
    for axis, dim in sides:
        count = lax.axis_size(axis)
        forward = [(i, i + 1) for i in range(count - 1)]
        backward = [(target, source) for source, target in forward]
        low = lax.ppermute(
            lax.slice_in_dim(block, block.shape[dim] - width, None, axis=dim), axis, forward
        )
        high = lax.ppermute(lax.slice_in_dim(block, 0, width, axis=dim), axis, backward)
        block = jnp.concatenate([low, block, high], axis=dim)
    return block


def build_mixer(whiten):
    half_band = BAND // 2
    rows_in = jnp.arange(CH_PROBE)[:, None, None]
    rows_out = jnp.arange(CH_PROBE)[None, :, None]
    offsets = jnp.arange(BAND)[None, None, :]
    selector = (rows_in - rows_out + half_band == offsets).astype(jnp.float32)
    per_probe = whiten.reshape(PROBES, CH_PROBE, BAND)
    mixer = jnp.einsum("poj,ioj->pio", per_probe, selector, precision=lax.Precision.HIGHEST)
    return mixer.astype(jnp.bfloat16)


def filter_rows(extended, out_rows, taps_b):
    ntaps = taps_b.shape[0]
    tile_rows = 128
    count = -(-out_rows // tile_rows)
    lag = jnp.arange(tile_rows + ntaps - 1)[None, :] - jnp.arange(tile_rows)[:, None]
    matches = lag[:, :, None] == jnp.arange(ntaps)[None, None, :]
    toeplitz = jnp.sum(
        jnp.where(matches, taps_b.astype(jnp.float32)[None, None, :], 0.0), axis=2
    ).astype(jnp.bfloat16)

    def one_tile(number):
        segment = lax.dynamic_slice_in_dim(extended, number * tile_rows, tile_rows + ntaps - 1, 0)
        return jnp.dot(toeplitz, segment, preferred_element_type=jnp.float32).astype(jnp.bfloat16)

    tiles = lax.map(one_tile, jnp.arange(count))
    return tiles.reshape(count * tile_rows, extended.shape[1])


def whiten_rows(filtered, mixer):
    count = filtered.shape[0]
    split = filtered.reshape(count, PROBES, CH_PROBE)
    mixed = jnp.einsum("npi,pio->npo", split, mixer, preferred_element_type=jnp.float32)
    return mixed.reshape(count, PROBES * CH_PROBE).astype(jnp.bfloat16)


def snippets(wide, spike_time, base):
    count = spike_time.shape[0]
    block_size = 128
    block_count = count // block_size
    width = wide.shape[1]
    sample_offsets = jnp.arange(TW)
    channels = jnp.arange(width)
    within = jnp.arange(NB)

    def one_block(number):
        spike_rows = lax.dynamic_slice_in_dim(spike_time, number * block_size, block_size, 0)
        starts = lax.dynamic_slice_in_dim(base, number * block_size, block_size, 0)
        row_index = (spike_rows[:, None] + sample_offsets[None, :]).reshape(block_size * TW)
        picked = jnp.take(wide, row_index, axis=0).reshape(block_size, TW, width)
        pick_cols = (
            channels[None, :, None] == starts[:, None, None] + within[None, None, :]
        ).astype(jnp.bfloat16)
        selected = jnp.einsum("stc,scv->stv", picked, pick_cols, preferred_element_type=jnp.float32)
        return selected.reshape(block_size, TW * NB).astype(jnp.bfloat16)

    blocks_out = lax.map(one_block, jnp.arange(block_count))
    return blocks_out.reshape(count, TW * NB)


def shards(
    raw,
    taps,
    whiten,
    templates,
    template_base,
    amp_scale,
    spike_time,
    spike_template,
    spike_session,
    live_count,
):
    rows = raw.shape[0]
    half_taps = taps.shape[0] // 2
    rim = TW // 2
    taps_b = taps.astype(jnp.bfloat16)
    mixer = build_mixer(whiten)
    position = lax.axis_index("tm")
    extended = padded(raw, (("tm", 0),), half_taps)
    white = whiten_rows(filter_rows(extended, rows, taps_b), mixer)
    wide = padded(white, (("tm", 0),), rim)
    base = template_base[spike_template]
    snippet = snippets(wide, spike_time, base).astype(jnp.float32)
    tmpl = templates.astype(jnp.float32)
    energy_t = jnp.sum(tmpl * tmpl, axis=1)
    chosen = tmpl[spike_template]
    inner = jnp.sum(snippet * chosen, axis=1)
    sessions = jnp.arange(amp_scale.shape[0])
    scale = jnp.sum(
        jnp.where(spike_session[:, None] == sessions[None, :], amp_scale[None, :], 0.0), axis=1
    )
    live = jnp.arange(spike_time.shape[0]) < live_count[0]
    amplitudes = jnp.where(live, scale * inner / (energy_t[spike_template] + 1e-05), 0.0)
    term = (amplitudes[:, None] * (snippet - amplitudes[:, None] * chosen)).astype(jnp.bfloat16)
    owners = jnp.arange(templates.shape[0])[:, None] == spike_template[None, :]
    selector = owners.astype(jnp.bfloat16)
    grads = jnp.dot(selector, term, preferred_element_type=jnp.float32)
    weight = jnp.sum(jnp.where(owners, (amplitudes * amplitudes)[None, :], 0.0), axis=1)
    owned = TEMP_DEV
    grads_mine, weight_mine = (
        lax.psum_scatter(grads, "tm", scatter_dimension=0, tiled=True),
        lax.psum_scatter(weight, "tm", scatter_dimension=0, tiled=True),
    )
    mine = lax.dynamic_slice_in_dim(tmpl, position * owned, owned, 0)
    new_templates = mine + grads_mine / (weight_mine[:, None] + 1.0)
    return (white, amplitudes, new_templates)


def solution(mesh):
    placed = (
        P("tm", "groups"),
        P(),
        P("groups", None),
        P("groups", None),
        P("groups"),
        P("groups"),
        P(("groups", "tm")),
        P(("groups", "tm")),
        P(("groups", "tm")),
        P(("groups", "tm")),
    )
    return jax.shard_map(
        shards,
        mesh=mesh,
        in_specs=placed,
        out_specs=(P("tm", "groups"), P(("groups", "tm")), P(("groups", "tm"), None)),
        check_vma=False,
    )
```

profile of v0, /device:TPU:0, one launch (start us, length us, event | category | flops | bytes accessed | tf_op | source)
XLA Modules:
  0.0 656.0 jit_solution(615177180178017248)
XLA Ops:
  16.3 10.7 %fusion.24 = bf16[4,384,384]{1,0,2:T(4,128)(2,1)S(1)} fusion(f32[4,384,33]{2,0,1:T(4,128)S(1)} %copy.38, s32[384,384]{0,1:T(8,128)} %subtract_add_fusion), kind=kOutput, calls=%fused_computation.40 | convolution fusion | flops 239026176 | bytes 1972224 | tf_op jit(solution)/shard_map/poj,ioj->pio/dot_general | solution.py:34
  27.3 32.2 %concatenate.6 = bf16[2108,1536]{1,0:T(8,128)(2,1)} concatenate(bf16[30,1536]{1,0:T(8,128)(2,1)S(1)} %collective-permute-done, bf16[2048,1536]{1,0:T(8,128)(2,1)} %param.14, bf16[30,1536]{1,0:T(8,128)(2,1)S(1)} %collective-permute-done.1), dimensions={0} | concatenate | bytes 12951552 | tf_op jit(solution)/shard_map/concatenate | solution.py:23
  59.6 55.9 %while.21 = (s32[]{:T(128)}, bf16[16,128,1536]{1,2,0:T(8,128)(2,1)}, s32[16]{0:T(128)S(1)}, bf16[2108,1536]{1,0:T(8,128)(2,1)}, bf16[128,188]{1,0:T(8,128)(2,1)S...) while((s32[]{:T(128)}, bf16[16,128,1536]{1,2,0:T(8,128)(2,1)}, s32[16]{0:T(128)S(1)}, ...), condition=%wide.region_2.3_spmd, body=%wide.region_1.2_spmd.sunk | while | flops 74121224 | bytes 1031835 | solution.py:52
  115.5 8.5 %copy.40 = bf16[16,128,1536]{1,0,2:T(8,128)(2,1)} copy(bf16[16,128,1536]{1,2,0:T(8,128)(2,1)} %get-tuple-element.77) | data formatting | bytes 12582912 | tf_op jit(solution)/shard_map/while | solution.py:52
  124.0 10.3 %reshape_reshape.3 = bf16[2048,4,384]{0,2,1:T(8,128)(2,1)} reshape(bf16[16,128,1536]{1,0,2:T(8,128)(2,1)} %copy.40) | data formatting | bytes 12582912 | tf_op jit(solution)/shard_map/reshape;reshape | solution.py:58
  134.3 6.5 convolution_convert_fusion.1
  151.6 6.9 %gather_fusion.1 = s32[1024]{0:T(1024)S(1)} fusion(s32[256]{0:T(256)S(1)} %copy-done, s32[1024]{0:T(1024)S(1)} %fusion.28), kind=kCustom, calls=%fused_computation.1 | custom fusion | bytes 12288 | tf_op jit(solution)/shard_map/gather | solution.py:108
  158.5 6.8 %gather_fusion.2 = f32[1024,2048]{1,0:T(8,128)} fusion(f32[256,2048]{1,0:T(8,128)S(1)} %convert_element_type.70, s32[1024]{0:T(1024)S(1)} %fusion.28), kind=kCustom, calls=%fused_computation.2 | custom fusion | bytes 16781312 | tf_op jit(solution)/shard_map/gather | solution.py:112
  165.3 9.1 %copy.46 = f32[8,128,2048]{1,2,0:T(8,128)} copy(f32[8,128,2048]{2,1,0:T(8,128)} %bitcast.58) | data formatting | bytes 16777216 | tf_op jit(solution)/shard_map/gather | solution.py:112
  174.4 11.3 %gather_fusion.3 = f32[1024]{0:T(1024)} fusion(f32[256]{0:T(256)S(1)} %multiply_reduce_fusion.1, s32[1024]{0:T(1024)S(1)} %fusion.28), kind=kCustom, calls=%fused_computation.3 | custom fusion | bytes 12288 | tf_op jit(solution)/shard_map/gather | solution.py:119
  186.3 8.6 %copy.48 = bf16[2048,1536]{1,0:T(8,128)(2,1)} copy(bf16[2048,1536]{0,1:T(8,128)(2,1)} %bitcast.61) | data formatting | bytes 12582912
  194.9 6.5 pad_maximum_fusion
  201.5 358.4 %while.22 = (s32[]{:T(128)}, bf16[8,128,2048]{1,2,0:T(8,128)(2,1)}, s32[8]{0:T(128)S(1)}, s32[1024]{0:T(1024)}, bf16[2080,1536]{1,0:T(8,128)(2,1)}, /*index=5*/s...) while((s32[]{:T(128)}, bf16[8,128,2048]{1,2,0:T(8,128)(2,1)}, s32[8]{0:T(128)S(1)}, ...), condition=%wide.region_5.6_spmd.clone, body=%wide.region_4.5_spmd.clone.sunk | while | flops 824500224 | bytes 40579240 | solution.py:83
  203.7 28.9 %gather_fusion = bf16[4096,1536]{1,0:T(8,128)(2,1)} fusion(bf16[2080,1536]{1,0:T(8,128)(2,1)} %get-tuple-element.259, s32[4096]{0:T(1024)S(1)} %broadcast_clamp_fusion.2), kind=kCustom, calls=%fused_computation.clone.clone.1 | custom fusion | bytes 25182208 | tf_op jit(solution)/shard_map/while/body/eval_jaxpr/jit(_take)/gather | solution.py:76
  232.9 11.4 %fusion.48 = bf16[128,32,64]{2,1,0:T(8,128)(2,1)S(1)} fusion(s32[128,64]{1,0:T(8,128)S(1)} %iota_add_fusion.4, bf16[128,32,1536]{2,1,0:T(8,128)(2,1)} %bitcast.57, pred[128,32]{1,0:T(8,128)(4,1)S(1)} %compare_and_fusion.2), kind=kOutput, calls=%fused_computation.18.clone.1 | convolution fusion | flops 824442880 | bytes 13144064 | tf_op jit(solution)/shard_map/while/body/eval_jaxpr/stc,scv->stv/dot_general | solution.py:80
  248.5 28.9 %gather_fusion = bf16[4096,1536]{1,0:T(8,128)(2,1)} fusion(bf16[2080,1536]{1,0:T(8,128)(2,1)} %get-tuple-element.259, s32[4096]{0:T(1024)S(1)} %broadcast_clamp_fusion.2), kind=kCustom, calls=%fused_computation.clone.clone.1 | custom fusion | bytes 25182208 | tf_op jit(solution)/shard_map/while/body/eval_jaxpr/jit(_take)/gather | solution.py:76
  277.7 11.4 %fusion.48 = bf16[128,32,64]{2,1,0:T(8,128)(2,1)S(1)} fusion(s32[128,64]{1,0:T(8,128)S(1)} %iota_add_fusion.4, bf16[128,32,1536]{2,1,0:T(8,128)(2,1)} %bitcast.57, pred[128,32]{1,0:T(8,128)(4,1)S(1)} %compare_and_fusion.2), kind=kOutput, calls=%fused_computation.18.clone.1 | convolution fusion | flops 824442880 | bytes 13144064 | tf_op jit(solution)/shard_map/while/body/eval_jaxpr/stc,scv->stv/dot_general | solution.py:80
  293.2 28.9 %gather_fusion = bf16[4096,1536]{1,0:T(8,128)(2,1)} fusion(bf16[2080,1536]{1,0:T(8,128)(2,1)} %get-tuple-element.259, s32[4096]{0:T(1024)S(1)} %broadcast_clamp_fusion.2), kind=kCustom, calls=%fused_computation.clone.clone.1 | custom fusion | bytes 25182208 | tf_op jit(solution)/shard_map/while/body/eval_jaxpr/jit(_take)/gather | solution.py:76
  322.4 11.4 %fusion.48 = bf16[128,32,64]{2,1,0:T(8,128)(2,1)S(1)} fusion(s32[128,64]{1,0:T(8,128)S(1)} %iota_add_fusion.4, bf16[128,32,1536]{2,1,0:T(8,128)(2,1)} %bitcast.57, pred[128,32]{1,0:T(8,128)(4,1)S(1)} %compare_and_fusion.2), kind=kOutput, calls=%fused_computation.18.clone.1 | convolution fusion | flops 824442880 | bytes 13144064 | tf_op jit(solution)/shard_map/while/body/eval_jaxpr/stc,scv->stv/dot_general | solution.py:80
  338.0 28.9 %gather_fusion = bf16[4096,1536]{1,0:T(8,128)(2,1)} fusion(bf16[2080,1536]{1,0:T(8,128)(2,1)} %get-tuple-element.259, s32[4096]{0:T(1024)S(1)} %broadcast_clamp_fusion.2), kind=kCustom, calls=%fused_computation.clone.clone.1 | custom fusion | bytes 25182208 | tf_op jit(solution)/shard_map/while/body/eval_jaxpr/jit(_take)/gather | solution.py:76
  367.3 11.4 %fusion.48 = bf16[128,32,64]{2,1,0:T(8,128)(2,1)S(1)} fusion(s32[128,64]{1,0:T(8,128)S(1)} %iota_add_fusion.4, bf16[128,32,1536]{2,1,0:T(8,128)(2,1)} %bitcast.57, pred[128,32]{1,0:T(8,128)(4,1)S(1)} %compare_and_fusion.2), kind=kOutput, calls=%fused_computation.18.clone.1 | convolution fusion | flops 824442880 | bytes 13144064 | tf_op jit(solution)/shard_map/while/body/eval_jaxpr/stc,scv->stv/dot_general | solution.py:80
  382.8 28.9 %gather_fusion = bf16[4096,1536]{1,0:T(8,128)(2,1)} fusion(bf16[2080,1536]{1,0:T(8,128)(2,1)} %get-tuple-element.259, s32[4096]{0:T(1024)S(1)} %broadcast_clamp_fusion.2), kind=kCustom, calls=%fused_computation.clone.clone.1 | custom fusion | bytes 25182208 | tf_op jit(solution)/shard_map/while/body/eval_jaxpr/jit(_take)/gather | solution.py:76
  412.0 11.4 %fusion.48 = bf16[128,32,64]{2,1,0:T(8,128)(2,1)S(1)} fusion(s32[128,64]{1,0:T(8,128)S(1)} %iota_add_fusion.4, bf16[128,32,1536]{2,1,0:T(8,128)(2,1)} %bitcast.57, pred[128,32]{1,0:T(8,128)(4,1)S(1)} %compare_and_fusion.2), kind=kOutput, calls=%fused_computation.18.clone.1 | convolution fusion | flops 824442880 | bytes 13144064 | tf_op jit(solution)/shard_map/while/body/eval_jaxpr/stc,scv->stv/dot_general | solution.py:80
  427.6 28.9 %gather_fusion = bf16[4096,1536]{1,0:T(8,128)(2,1)} fusion(bf16[2080,1536]{1,0:T(8,128)(2,1)} %get-tuple-element.259, s32[4096]{0:T(1024)S(1)} %broadcast_clamp_fusion.2), kind=kCustom, calls=%fused_computation.clone.clone.1 | custom fusion | bytes 25182208 | tf_op jit(solution)/shard_map/while/body/eval_jaxpr/jit(_take)/gather | solution.py:76
  456.9 11.4 %fusion.48 = bf16[128,32,64]{2,1,0:T(8,128)(2,1)S(1)} fusion(s32[128,64]{1,0:T(8,128)S(1)} %iota_add_fusion.4, bf16[128,32,1536]{2,1,0:T(8,128)(2,1)} %bitcast.57, pred[128,32]{1,0:T(8,128)(4,1)S(1)} %compare_and_fusion.2), kind=kOutput, calls=%fused_computation.18.clone.1 | convolution fusion | flops 824442880 | bytes 13144064 | tf_op jit(solution)/shard_map/while/body/eval_jaxpr/stc,scv->stv/dot_general | solution.py:80
  472.5 28.9 %gather_fusion = bf16[4096,1536]{1,0:T(8,128)(2,1)} fusion(bf16[2080,1536]{1,0:T(8,128)(2,1)} %get-tuple-element.259, s32[4096]{0:T(1024)S(1)} %broadcast_clamp_fusion.2), kind=kCustom, calls=%fused_computation.clone.clone.1 | custom fusion | bytes 25182208 | tf_op jit(solution)/shard_map/while/body/eval_jaxpr/jit(_take)/gather | solution.py:76
  501.7 11.4 %fusion.48 = bf16[128,32,64]{2,1,0:T(8,128)(2,1)S(1)} fusion(s32[128,64]{1,0:T(8,128)S(1)} %iota_add_fusion.4, bf16[128,32,1536]{2,1,0:T(8,128)(2,1)} %bitcast.57, pred[128,32]{1,0:T(8,128)(4,1)S(1)} %compare_and_fusion.2), kind=kOutput, calls=%fused_computation.18.clone.1 | convolution fusion | flops 824442880 | bytes 13144064 | tf_op jit(solution)/shard_map/while/body/eval_jaxpr/stc,scv->stv/dot_general | solution.py:80
  517.3 28.9 %gather_fusion = bf16[4096,1536]{1,0:T(8,128)(2,1)} fusion(bf16[2080,1536]{1,0:T(8,128)(2,1)} %get-tuple-element.259, s32[4096]{0:T(1024)S(1)} %broadcast_clamp_fusion.2), kind=kCustom, calls=%fused_computation.clone.clone.1 | custom fusion | bytes 25182208 | tf_op jit(solution)/shard_map/while/body/eval_jaxpr/jit(_take)/gather | solution.py:76
  546.5 11.4 %fusion.48 = bf16[128,32,64]{2,1,0:T(8,128)(2,1)S(1)} fusion(s32[128,64]{1,0:T(8,128)S(1)} %iota_add_fusion.4, bf16[128,32,1536]{2,1,0:T(8,128)(2,1)} %bitcast.57, pred[128,32]{1,0:T(8,128)(4,1)S(1)} %compare_and_fusion.2), kind=kOutput, calls=%fused_computation.18.clone.1 | convolution fusion | flops 824442880 | bytes 13144064 | tf_op jit(solution)/shard_map/while/body/eval_jaxpr/stc,scv->stv/dot_general | solution.py:80
  559.8 7.2 %copy.47 = f32[8,128,2048]{2,1,0:T(8,128)} copy(bf16[8,128,2048]{1,2,0:T(8,128)(2,1)} %get-tuple-element.78) | data formatting | bytes 12582912 | tf_op jit(solution)/shard_map/convert_element_type | solution.py:109
  582.6 35.0 %all-reduce = f32[256]{0:T(256)S(1)} all-reduce(f32[256]{0:T(256)S(1)} %select_reduce_fusion.1), channel_id=3, replica_groups=mesh['groups'=2,'tm'=16] {'tm'}, use_global_device_ids=true, to_apply=%region_10.11.clone | all-reduce | flops 256 | bytes 2048
  617.7 29.7 %reduce-scatter.2.cloned.1.call-done = f32[16,2048]{1,0:T(8,128)} async-done(((f32[256,2048]{1,0:T(8,128)}), f32[16,2048]{1,0:T(8,128)}) %reduce-scatter.2.cloned.1.call-update) | async-done | bytes 131088 | tf_op jit(solution)/shard_map/reduce_scatter | solution.py:127
  (183 shorter events, 112.4 us)
Async XLA Ops:
  7.2 144.4 %copy-start = (s32[256]{0:T(256)S(1)}, s32[256]{0:T(256)}, u32[]{:S(2)}) copy-start(s32[256]{0:T(256)} %param.18) | copy-start | bytes 3076
  7.2 640.3 %reduce-scatter.2.cloned.1.call-start = ((), (), s32[]{:S(2)}) async-start(), calls=%async_computation.1 | async-start | bytes 2228224 | tf_op jit(solution)/shard_map/reduce_scatter | solution.py:127
  8.2 19.1 %collective-permute-start = (bf16[30,1536]{1,0:T(8,128)(2,1)S(1)}, bf16[30,1536]{1,0:T(8,128)(2,1)S(1)}, u32[]{:S(2)}, u32[]{:S(2)}) collective-permute-start(bf16[30,1536]{1,0:T(8,128)(2,1)S(1)} %get-tuple-element.139), channel_id=1, source_target_pairs={{0,1},{1,2},{2,3},{3,4},{4,5},{5,6},{6,7},{7,8},{8,9},{9,10},{10,1... | collective-permute-start | bytes 276488 | tf_op jit(solution)/shard_map/ppermute | solution.py:19
  10.6 16.7 %collective-permute-start.1 = (bf16[30,1536]{1,0:T(8,128)(2,1)S(1)}, bf16[30,1536]{1,0:T(8,128)(2,1)S(1)}, u32[]{:S(2)}, u32[]{:S(2)}) collective-permute-start(bf16[30,1536]{1,0:T(8,128)(2,1)S(1)} %get-tuple-element.138), channel_id=1, source_target_pairs={{1,0},{2,1},{3,2},{4,3},{5,4},{6,5},{7,6},{8,7},{9,8},{10,9},{11,1... | collective-permute-start | bytes 276488 | tf_op jit(solution)/shard_map/ppermute | solution.py:22
  16.3 10.7 %copy-start.5 = (bf16[256,2048]{1,0:T(8,128)(2,1)S(1)}, bf16[256,2048]{1,0:T(8,128)(2,1)}, u32[]{:S(2)}) copy-start(bf16[256,2048]{1,0:T(8,128)(2,1)} %param.17) | copy-start | bytes 3145732
  134.3 16.4 %copy-start.10 = (s32[1024]{0:T(1024)S(1)}, s32[1024]{0:T(1024)}, u32[]{:S(2)}) copy-start(s32[1024]{0:T(1024)} %param.22) | copy-start | bytes 12292
  134.3 16.4 %copy-start.11 = (f32[8]{0:T(128)S(1)}, f32[8]{0:T(128)}, u32[]{:S(2)}) copy-start(f32[8]{0:T(128)} %param.19) | copy-start | bytes 100
  140.8 2.7 copy-start.4
  143.8 51.1 %collective-permute-start.2 = (bf16[16,1536]{1,0:T(8,128)(2,1)S(1)}, bf16[16,1536]{1,0:T(8,128)(2,1)S(1)}, u32[]{:S(2)}, u32[]{:S(2)}) collective-permute-start(bf16[16,1536]{1,0:T(8,128)(2,1)S(1)} %copy.43), channel_id=1, source_target_pairs={{0,1},{1,2},{2,3},{3,4},{4,5},{5,6},{6,7},{7,8},{8,9},{9,10},{10,1... | collective-permute-start | bytes 147464 | tf_op jit(solution)/shard_map/ppermute | solution.py:19
  149.2 45.8 %collective-permute-start.3 = (bf16[16,1536]{1,0:T(8,128)(2,1)S(1)}, bf16[16,1536]{1,0:T(8,128)(2,1)S(1)}, u32[]{:S(2)}, u32[]{:S(2)}) collective-permute-start(bf16[16,1536]{1,0:T(8,128)(2,1)S(1)} %copy.44), channel_id=1, source_target_pairs={{1,0},{2,1},{3,2},{4,3},{5,4},{6,5},{7,6},{8,7},{9,8},{10,9},{11,1... | collective-permute-start | bytes 147464 | tf_op jit(solution)/shard_map/ppermute | solution.py:22
  151.6 13.7 %copy-start.2 = (f32[256,2048]{1,0:T(8,128)}, f32[256,2048]{1,0:T(8,128)S(1)}, u32[]{:S(2)}) copy-start(f32[256,2048]{1,0:T(8,128)S(1)} %convert_element_type.70) | copy-start | bytes 6291460
  567.0 5.6 copy-start.7
  567.0 5.6 copy-start.8
  567.0 7.0 %copy-start.3 = (f32[1024,2048]{1,0:T(8,128)S(1)}, f32[1024,2048]{1,0:T(8,128)}, u32[]{:S(2)}) copy-start(f32[1024,2048]{1,0:T(8,128)} %gather_fusion.2) | copy-start | bytes 25165828
  572.6 5.9 copy-start.9
  574.0 4.5 copy-start.6
  574.0 75.1 %copy-start.1 = (s32[256]{0:T(256)S(1)}, s32[256]{0:T(256)}, u32[]{:S(2)}) copy-start(s32[256]{0:T(256)} %param.18) | copy-start | bytes 3076
  578.5 2.7 copy-start.12
Sparse Core Ops, SparseCore 0:
  581.3 66.0 reduce-scatter.1
where the time goes:
time: 660 us; the launch traced here: 656 us
  local copies, waits for them, and re-layouts  377 us (57%)
  matrix products  147 us (22%)
  blocking collectives  35 us (5%)
  waiting for transfers between devices  29.8 us (5%)
  other arithmetic  24.9 us (4%)
  loops' own time  15.9 us (2%)
  between operations  15.6 us (2%)
  starting transfers between devices  10.3 us (2%)
    gather x8, local copies, waits for them, and re-layouts, one_block(): picked = jnp.take(wide, row_index, axis=0).reshape(block_size, TW, width)  232 us
    dot_general x8, matrix products, one_block(): jnp.einsum('stc,scv->stv', picked, pick_cols, preferred_element_type=jnp....  91.2 us
    dot_general x16, matrix products, one_tile(): jnp.dot(toeplitz, segment, preferred_element_type=jnp.float32)  36.1 us
    unnamed x1, blocking collectives  35 us
    concatenate x1, local copies, waits for them, and re-layouts, padded(): block = jnp.concatenate([low, block, high], axis=dim)  32.2 us
    reduce_scatter x1, waiting for transfers between devices, shards(): lax.psum_scatter(grads, 'tm', scatter_dimension=0, tiled=True)  29.7 us
    gather x2, local copies, waits for them, and re-layouts, shards(): chosen = tmpl[spike_template]  15.9 us
    unnamed x28, local copies, waits for them, and re-layouts  13.3 us
  transfers between devices with their start and end apart: 5, of which 1 were waited for; matrix products, arithmetic and copies ran while one was open for 9% of the time, Pallas kernels for 0%

commit v1 on v0

v1 whole, which is shorter than its diff:
```python
import jax
import jax.numpy as jnp
from jax import lax
from jax.experimental import pallas as pl
from jax.experimental.pallas import tpu as pltpu
from jax.sharding import PartitionSpec as P

CH_PROBE = 384
BAND = 33
TW = 32
NB = 64
TEMP_DEV = 16
CAP = 8
TILE = 256
HALO = 48
GROUP = 16
PACK = CAP * TW // 2 + 2 * CAP


def from_neighbours(low_part, high_part, axis):
    count = lax.axis_size(axis)
    forward = [(i, i + 1) for i in range(count - 1)]
    backward = [(target, source) for source, target in forward]
    return lax.ppermute(low_part, axis, forward), lax.ppermute(high_part, axis, backward)


def body(
    time_s,
    tmpl_s,
    slot_s,
    quot_s,
    rest_s,
    used_s,
    edge_s,
    raw_ref,
    prev_ref,
    next_ref,
    low_ref,
    high_ref,
    taps_ref,
    whiten_ref,
    temp_ref,
    coef_ref,
    white_ref,
    amp_ref,
    pack_ref,
    wide,
    toep,
    mixer,
    placed,
    sums,
    squares,
):
    i = pl.program_id(0)
    last = pl.num_programs(0) - 1
    width = raw_ref.shape[1]
    lanes = width // 128
    probes = width // CH_PROBE
    slots = placed.shape[0]
    rows = wide.shape[1] - TW

    lane = lax.broadcasted_iota(jnp.int32, (TW, 128), 1)

    @pl.when(i == 0)
    def _():
        spread = jnp.broadcast_to(taps_ref[...], (TILE, taps_ref.shape[1]))
        skewed = pltpu.roll(spread, 0, 1, stride=1, stride_axis=0)
        toep[...] = skewed.astype(jnp.bfloat16)
        for p in range(probes):
            part = whiten_ref[p * CH_PROBE : (p + 1) * CH_PROBE, :]
            part = jnp.concatenate([part, jnp.zeros((CH_PROBE, 384), jnp.float32)], axis=1)
            skewed = pltpu.roll(part, 512 - BAND // 2, 1, stride=1, stride_axis=0)
            mixer[p] = skewed[:, :CH_PROBE].T.astype(jnp.bfloat16)

    def whitened(segment, band):
        filtered = jnp.dot(band, segment, preferred_element_type=jnp.float32).astype(jnp.bfloat16)
        return [
            jnp.dot(
                filtered[:, p * CH_PROBE : (p + 1) * CH_PROBE],
                mixer[p],
                preferred_element_type=jnp.float32,
            ).astype(jnp.bfloat16)
            for p in range(probes)
        ]

    def keep(parts, start, size, scale=None):
        whole = jnp.concatenate(parts, axis=1).astype(jnp.float32)
        if scale is not None:
            whole = whole * scale
        for c in range(lanes):
            wide[c, pl.ds(start, size), :] = whole[:, c * 128 : (c + 1) * 128]

    prev = jnp.where(i == 0, low_ref[HALO - 32 :, :], prev_ref[...])
    after = jnp.where(i == last, high_ref[:32, :], next_ref[...])
    segment = jnp.concatenate([prev, raw_ref[...], after], axis=0)
    parts = whitened(segment, toep[:, : TILE + 64])
    for p in range(probes):
        white_ref[:, p * CH_PROBE : (p + 1) * CH_PROBE] = parts[p]
    keep(parts, pl.multiple_of(16 + i * TILE, 16), TILE)

    @pl.when(i == 0)
    def _():
        segment = jnp.concatenate([low_ref[...], raw_ref[:32, :]], axis=0)
        inside = edge_s[0].astype(jnp.float32)
        keep(whitened(segment, toep[:16, : HALO + 32]), 0, 16, inside)

    @pl.when(i == last)
    def _():
        segment = jnp.concatenate([raw_ref[TILE - 32 :, :], high_ref[...]], axis=0)
        inside = edge_s[1].astype(jnp.float32)
        keep(whitened(segment, toep[:16, : HALO + 32]), rows + 16, 16, inside)

        @pl.loop(0, slots // 4)
        def _(four):
            for j in range(4):
                slot = four * 4 + j
                k = used_s[slot]
                r = rest_s[k]
                rolled = pltpu.roll(temp_ref[k].astype(jnp.float32), lax.rem(r, 128), 1)
                for half in range(2):
                    at = lane + 128 * half - r
                    placed[slot, half] = jnp.where((at >= 0) & (at < NB), rolled, 0.0)
                    sums[slot, half] = jnp.zeros((TW, 128), jnp.float32)

        squares[...] = jnp.zeros_like(squares)

        @pl.loop(0, amp_ref.shape[0] // GROUP)
        def _(group):
            first = pl.multiple_of(group * GROUP, GROUP)
            windows, places, folded = [], [], []
            for j in range(GROUP):
                k = tmpl_s[first + j]
                slot = slot_s[k]
                window = wide[pl.ds(quot_s[k], 2), pl.ds(time_s[first + j], TW), :]
                product = window * placed[slot]
                total = product[0] + product[1]
                folded.append(jnp.sum(total, axis=0, keepdims=True))
                windows.append(window)
                places.append(slot)
            inner = jnp.sum(jnp.concatenate(folded, axis=0), axis=1, keepdims=True)
            amps = coef_ref[pl.ds(first, GROUP), :] * inner
            amp_ref[pl.ds(first, GROUP), :] = amps
            for j in range(GROUP):
                one = amps[j : j + 1, :]
                sums[places[j]] += one[None] * windows[j]
                squares[pl.ds(places[j], 1), :] += jnp.broadcast_to(one * one, (1, 128))

        half_lane = lane[: TW // 2]
        aux_lane = lane[:CAP]
        aux_row = lax.broadcasted_iota(jnp.int32, (CAP, 128), 0)

        @pl.loop(0, slots // CAP)
        def _(owner):
            start = pl.multiple_of(owner * PACK, 16)
            names = jnp.zeros((CAP, 128), jnp.float32)
            for j in range(CAP):
                slot = owner * CAP + j
                k = used_s[slot]
                r = rest_s[k]
                merged = jnp.where(lane >= r, sums[slot, 0], sums[slot, 1])
                merged = jnp.where(r >= 128, sums[slot, 1], merged)
                back = pltpu.roll(merged, lax.rem(256 - r, 128), 1)
                lower = back[TW // 2 :]
                both = jnp.where(half_lane < NB, back[: TW // 2], pltpu.roll(lower, NB, 1))
                pack_ref[pl.ds(pl.multiple_of(start + j * 16, 16), 16), :] = both.astype(
                    jnp.bfloat16
                )
                name = (k - owner * TEMP_DEV).astype(jnp.float32)
                names = jnp.where(aux_row == j, name, names)
            aux = squares[pl.ds(pl.multiple_of(owner * CAP, CAP), CAP), :]
            aux = jnp.where(aux_lane == 1, names, aux)
            high = aux.astype(jnp.bfloat16)
            rest = (aux - high.astype(jnp.float32)).astype(jnp.bfloat16)
            both = jnp.concatenate([high.astype(jnp.float32), rest.astype(jnp.float32)], axis=0)
            pack_ref[pl.ds(pl.multiple_of(start + CAP * 16, 16), 16), :] = both.astype(jnp.bfloat16)


def shards(
    raw,
    taps,
    whiten,
    templates,
    template_base,
    amp_scale,
    spike_time,
    spike_template,
    spike_session,
    live_count,
):
    rows, width = raw.shape
    spikes = spike_time.shape[0]
    ntemp = templates.shape[0]
    position = lax.axis_index("tm")
    owners = lax.axis_size("tm")
    slots = owners * CAP
    low, high = from_neighbours(raw[rows - HALO :], raw[:HALO], "tm")
    edges = jnp.stack([position > 0, position < owners - 1]).astype(jnp.int32)

    taps_b = taps.astype(jnp.bfloat16).astype(jnp.float32)
    taps_row = jnp.pad(taps_b, (2, 384 - 2 - taps.shape[0]))[None, :]
    whiten_wide = jnp.pad(whiten, ((0, 0), (0, 128 - BAND)))
    temp_wide = jnp.pad(templates.reshape(ntemp, TW, NB), ((0, 0), (0, 0), (0, 128 - NB)))
    quot = jnp.minimum(template_base // 128, width // 128 - 2)
    rest = template_base - quot * 128

    tmpl = templates.astype(jnp.float32)
    energy_t = jnp.sum(tmpl * tmpl, axis=1)
    named = spike_template[:, None] == jnp.arange(ntemp)[None, :]
    energy = jnp.sum(jnp.where(named, energy_t[None, :], 0.0), axis=1)
    present = jnp.any(named, axis=0).reshape(owners, TEMP_DEV)
    local = jnp.arange(TEMP_DEV)
    before = local[:, None] < local[None, :]
    rank = jnp.sum(jnp.where(before[None], present[:, :, None].astype(jnp.int32), 0), axis=1)
    owner_ids = jnp.arange(owners)
    slot_of = jnp.where(present, owner_ids[:, None] * CAP + rank, 0).reshape(ntemp)
    hits = present[:, None, :] & (rank[:, None, :] == jnp.arange(CAP)[None, :, None])
    used = jnp.sum(jnp.where(hits, local[None, None, :], 0), axis=2)
    used = (used + owner_ids[:, None] * TEMP_DEV).reshape(slots)

    sessions = jnp.arange(amp_scale.shape[0])
    scale = jnp.sum(
        jnp.where(spike_session[:, None] == sessions[None, :], amp_scale[None, :], 0.0), axis=1
    )
    live = jnp.arange(spikes) < live_count[0]
    coef = jnp.where(live, scale / (energy + 1e-05), 0.0)[:, None]

    step = TILE // 32
    final = rows // 32 - 1
    fixed2 = lambda i, *_: (0, 0)
    white, amps, packed = pl.pallas_call(
        body,
        grid_spec=pltpu.PrefetchScalarGridSpec(
            num_scalar_prefetch=7,
            grid=(rows // TILE,),
            in_specs=[
                pl.BlockSpec((TILE, width), lambda i, *_: (i, 0)),
                pl.BlockSpec((32, width), lambda i, *_: (jnp.maximum(i * step - 1, 0), 0)),
                pl.BlockSpec((32, width), lambda i, *_: (jnp.minimum((i + 1) * step, final), 0)),
                pl.BlockSpec((HALO, width), fixed2),
                pl.BlockSpec((HALO, width), fixed2),
                pl.BlockSpec((1, 384), fixed2),
                pl.BlockSpec((width, 128), fixed2),
                pl.BlockSpec((ntemp, TW, 128), lambda i, *_: (0, 0, 0)),
                pl.BlockSpec((spikes, 1), fixed2),
            ],
            out_specs=[
                pl.BlockSpec((TILE, width), lambda i, *_: (i, 0)),
                pl.BlockSpec((spikes, 1), fixed2),
                pl.BlockSpec((owners * PACK, 128), fixed2),
            ],
            scratch_shapes=[
                pltpu.VMEM((width // 128, rows + TW, 128), jnp.float32),
                pltpu.VMEM((TILE, 384), jnp.bfloat16),
                pltpu.VMEM((width // CH_PROBE, CH_PROBE, CH_PROBE), jnp.bfloat16),
                pltpu.VMEM((slots, 2, TW, 128), jnp.float32),
                pltpu.VMEM((slots, 2, TW, 128), jnp.float32),
                pltpu.VMEM((slots, 128), jnp.float32),
            ],
        ),
        out_shape=[
            jax.ShapeDtypeStruct((rows, width), jnp.bfloat16),
            jax.ShapeDtypeStruct((spikes, 1), jnp.float32),
            jax.ShapeDtypeStruct((owners * PACK, 128), jnp.bfloat16),
        ],
        compiler_params=pltpu.CompilerParams(
            dimension_semantics=("arbitrary",), vmem_limit_bytes=56 * 1024 * 1024
        ),
    )(
        spike_time,
        spike_template,
        slot_of,
        quot,
        rest,
        used,
        edges,
        raw,
        raw,
        raw,
        low,
        high,
        taps_row,
        whiten_wide,
        temp_wide,
        coef,
    )

    arrived = lax.all_to_all(packed.reshape(owners, PACK, 128), "tm", 0, 0)
    body_rows = CAP * TW // 2
    grads = arrived[:, :body_rows].reshape(owners * CAP, TW // 2 * 128)
    aux = arrived[:, body_rows:, :2].astype(jnp.float32).reshape(owners, 2, CAP, 2)
    weight = (aux[:, 0, :, 0] + aux[:, 1, :, 0]).reshape(slots)
    names = aux[:, 0, :, 1].reshape(slots).astype(jnp.int32)
    pick = local[:, None] == names[None, :]
    total = jnp.dot(pick.astype(jnp.bfloat16), grads, preferred_element_type=jnp.float32)
    total = total.reshape(TEMP_DEV, TW // 2, 2, NB).transpose(0, 2, 1, 3)
    total = total.reshape(TEMP_DEV, TW * NB)
    weights = jnp.sum(jnp.where(pick, weight[None, :], 0.0), axis=1)
    mine = lax.dynamic_slice_in_dim(templates, position * TEMP_DEV, TEMP_DEV, 0)
    new_templates = (mine.astype(jnp.float32) + total) / (weights[:, None] + 1.0)
    return white, amps.reshape(spikes), new_templates


def solution(mesh):
    placed = (
        P("tm", "groups"),
        P(),
        P("groups", None),
        P("groups", None),
        P("groups"),
        P("groups"),
        P(("groups", "tm")),
        P(("groups", "tm")),
        P(("groups", "tm")),
        P(("groups", "tm")),
    )
    return jax.shard_map(
        shards,
        mesh=mesh,
        in_specs=placed,
        out_specs=(P("tm", "groups"), P(("groups", "tm")), P(("groups", "tm"), None)),
        check_vma=False,
    )
```

time: 660 us -> 94.8 us (0.14)
  local copies, waits for them, and re-layouts: 377 us -> 15.7 us
  matrix products: 147 us -> 0.51 us
  Pallas kernels: 0 us -> 39.9 us
  blocking collectives: 35 us -> 0 us
  waiting for transfers between devices: 29.8 us -> 13.7 us
  loops' own time: 15.9 us -> 0 us
  other arithmetic: 24.9 us -> 10.5 us
  between operations: 15.6 us -> 1.48 us
    gather x12 -> x0, local copies, waits for them, and re-layouts: 266 us -> none  [the longest x8 232 us: one_block(): picked = jnp.take(wide, row_index, axis=0).reshape(block_size, TW, width)]
    dot_general x27 -> x1, matrix products: 147 us -> 0.51 us  [shards(): jnp.dot(pick.astype(jnp.bfloat16), grads, preferred_element_type=jnp.floa...]
    pallas_call x0 -> x1, Pallas kernels: none -> 39.9 us  [shards(): pl.pallas_call(body, grid_spec=pltpu.PrefetchScalarGridSpec(num_scalar_pr...]
    unnamed x1 -> x0, blocking collectives: 35 us -> none
    concatenate x1 -> x0, local copies, waits for them, and re-layouts: 32.2 us -> none  [padded(): block = jnp.concatenate([low, block, high], axis=dim)]
    reduce_scatter x1 -> x0, waiting for transfers between devices: 29.7 us -> none  [shards(): lax.psum_scatter(grads, 'tm', scatter_dimension=0, tiled=True)]
    dynamic_slice x40 -> x0, local copies, waits for them, and re-layouts: 20.8 us -> none  [the longest x16 9.32 us: filter_rows(): tiles = lax.map(one_tile, jnp.arange(count))]
    convert_element_type x9 -> x2, local copies, waits for them, and re-layouts: 16.3 us -> 0.16 us  [shards(): names = aux[:, 0, :, 1].reshape(slots).astype(jnp.int32)]
  transfers between devices with their start and end apart: 5 -> 3, of which waited for: 1 -> 1; matrix products, arithmetic and copies ran while one was open for 9% -> 23% of each run, Pallas kernels for 0% -> 0%
where the time goes in v1:
time: 94.8 us; the launch traced here: 94 us
  Pallas kernels  39.9 us (42%)
  local copies, waits for them, and re-layouts  15.7 us (17%)
  waiting for transfers between devices  13.7 us (14%)
  starting transfers between devices  12.3 us (13%)
  other arithmetic  10.5 us (11%)
  between operations  1.48 us (2%)
    pallas_call x1, Pallas kernels, shards(): pl.pallas_call(body, grid_spec=pltpu.PrefetchScalarGridSpec(num_scalar_pr...  39.9 us
    all_to_all x1, waiting for transfers between devices, shards(): arrived = lax.all_to_all(packed.reshape(owners, PACK, 128), 'tm', 0, 0)  13.7 us
    all_to_all x1, starting transfers between devices, shards(): arrived = lax.all_to_all(packed.reshape(owners, PACK, 128), 'tm', 0, 0)  7.95 us
    reshape x1, local copies, waits for them, and re-layouts, shards(): templates.reshape(ntemp, TW, NB)  3.91 us
    unnamed x13, local copies, waits for them, and re-layouts  3.39 us
    ppermute x1, starting transfers between devices, from_neighbours(): lax.ppermute(low_part, axis, forward)  3.04 us
    pad x1, local copies, waits for them, and re-layouts, shards(): whiten_wide = jnp.pad(whiten, ((0, 0), (0, 128 - BAND)))  2.1 us
  transfers between devices with their start and end apart: 3, of which 1 were waited for; matrix products, arithmetic and copies ran while one was open for 23% of the time, Pallas kernels for 0%

profile of v1, /device:TPU:0, one launch (start us, length us, event | category | flops | bytes accessed | tf_op | source)
XLA Modules:
  0.0 94.0 jit_solution(3503799295554410261)
XLA Ops:
  0.7 1.8 %fusion.8 = (bf16[48,1536]{1,0:T(8,128)(2,1)}, bf16[48,1536]{1,0:T(8,128)(2,1)}) fusion(bf16[2048,1536]{1,0:T(8,128)(2,1)} %next_ref.1), kind=kLoop, calls=%fused_computation.37 | loop fusion | bytes 589824 | tf_op jit(solution)/shard_map/slice | solution.py:196
  2.5 1.3 %collective-permute-start.1 = (bf16[48,1536]{1,0:T(8,128)(2,1)}, bf16[48,1536]{1,0:T(8,128)(2,1)S(1)}, u32[]{:S(2)}, u32[]{:S(2)}) collective-permute-start(bf16[48,1536]{1,0:T(8,128)(2,1)} %get-tuple-element.11), channel_id=1, source_target_pairs={{1,0},{2,1},{3,2},{4,3},{5,4},{6,5},{7,6},{8,7},{9,8},{10,9},{11,1... | collective-permute-start | bytes 442376 | tf_op jit(solution)/shard_map/ppermute | solution.py:24
  3.8 3.0 %collective-permute-start = (bf16[48,1536]{1,0:T(8,128)(2,1)}, bf16[48,1536]{1,0:T(8,128)(2,1)S(1)}, u32[]{:S(2)}, u32[]{:S(2)}) collective-permute-start(bf16[48,1536]{1,0:T(8,128)(2,1)} %get-tuple-element.12), channel_id=1, source_target_pairs={{0,1},{1,2},{2,3},{3,4},{4,5},{5,6},{6,7},{7,8},{8,9},{9,10},{10,1... | collective-permute-start | bytes 442376 | tf_op jit(solution)/shard_map/ppermute | solution.py:24
  7.5 0.9 fusion
  8.4 0.7 convert_element_type.41
  9.1 1.5 %multiply_reduce_fusion = f32[256]{0:T(256)S(1)} fusion(bf16[256,2048]{1,0:T(8,128)(2,1)} %param.13), kind=kLoop, calls=%fused_computation | loop fusion | flops 1572608 | bytes 1049600 | tf_op jit(solution)/shard_map/reduce_sum | solution.py:207
  10.7 1.1 %select_reduce_fusion = f32[1024]{0:T(1024)S(1)} fusion(f32[256]{0:T(256)S(1)} %multiply_reduce_fusion, s32[1024]{0:T(1024)} %tmpl_s.1), kind=kLoop, calls=%fused_computation.2 | loop fusion | flops 785408 | bytes 9216 | tf_op jit(solution)/shard_map/reduce_sum | solution.py:209
  11.9 0.3 select_reduce_fusion.2
  12.4 0.8 select_reduce_fusion.3
  13.2 0.2 copy.45
  13.5 0.6 multiply_subtract_fusion
  14.1 0.8 fusion.1.coef_ref
  15.0 1.3 %copy.43 = bf16[256,2048]{0,1:T(8,128)(2,1)} copy(bf16[256,2048]{1,0:T(8,128)(2,1)S(1)} %copy-done) | data formatting | bytes 2097152 | tf_op args[3]
  16.3 0.6 reshape.127.taps_ref
  16.9 0.7 add.74.used_s
  17.5 1.2 %copy.42 = f32[1536,33]{1,0:T(8,128)} copy(f32[1536,33]{0,1:T(8,128)S(1)} %copy-done.1) | data formatting | bytes 405504 | tf_op args[2]
  18.7 3.9 %copy.44 = bf16[256,32,64]{2,1,0:T(8,128)(2,1)S(1)} copy(bf16[256,32,64]{0,2,1:T(8,128)(2,1)} %bitcast.30) | data formatting | bytes 2097152 | tf_op jit(solution)/shard_map/reshape | solution.py:202
  22.6 2.1 %pad.14.whiten_ref = f32[1536,128]{1,0:T(8,128)} pad(f32[1536,33]{1,0:T(8,128)} %copy.42, f32[]{:T(128)} %constant.42.clone.1), padding=0_0x0_95 | pad | bytes 989188 | tf_op jit(solution)/shard_map/jit(_pad)/pad | solution.py:201
  24.7 1.8 %pad.15.temp_ref = bf16[256,32,128]{2,1,0:T(8,128)(2,1)} pad(bf16[256,32,64]{2,1,0:T(8,128)(2,1)S(1)} %copy.44, bf16[]{:T(256)} %constant.41.clone.1), padding=0_0x0_0x0_64 | pad | bytes 3145730 | tf_op jit(solution)/shard_map/jit(_pad)/pad | solution.py:202
  26.5 0.7 add_convert_fusion.edge_s
  27.2 0.6 copy-done.2
  27.9 39.9 %shard_map.121 = (bf16[2048,1536]{1,0:T(8,128)(2,1)}, f32[1024,1]{1,0:T(8,128)}, bf16[2304,128]{1,0:T(8,128)(2,1)}) custom-call(s32[1024]{0:T(1024)} %time_s.1, s32[1024]{0:T(1024)} %tmpl_s.1, s32[256]{0:T(256)} %get-tuple-element.15.slot_s, s32[256]{0:T(256)} %get-tuple-element.10.quot_s, s32[256]{0:T(256)} %get-tuple-element.9.rest_s, s32[128]{0:T(128)} %add.74.used_s, ...), custom_call_target="tpu_custom_call" | custom-call | tf_op jit(solution)/shard_map/pallas_call | solution.py:230
  67.8 8.0 %all-to-all-start = ((bf16[16,144,128]{2,1,0:T(8,128)(2,1)}), bf16[16,144,128]{2,1,0:T(8,128)(2,1)S(1)}, u32[]{:S(2)}, u32[]{:S(2)}) async-start(bf16[16,144,128]{2,1,0:T(8,128)(2,1)} %bitcast.33), calls=%async_computation | async-start | bytes 1179648 | tf_op jit(solution)/shard_map/all_to_all | solution.py:287
  75.7 1.8 %reduce = f32[1024]{0:T(1024)} reduce(f32[1024,1]{1,0:T(8,128)} %get-tuple-element.7, f32[]{:T(128)} %constant.53), dimensions={1}, to_apply=%get-tuple-element.7.reduce_sub_computation | reduce | bytes 8196 | tf_op jit(solution)/shard_map/pallas_call | solution.py:230
  77.6 13.7 %all-to-all-done = bf16[16,144,128]{2,1,0:T(8,128)(2,1)S(1)} async-done(((bf16[16,144,128]{2,1,0:T(8,128)(2,1)}), bf16[16,144,128]{2,1,0:T(8,128)(2,1)S(1)}, u32[]{:S(2)}, u32[]{:S(2)}) %all-to-all-start) | async-done | bytes 589856 | tf_op jit(solution)/shard_map/all_to_all | solution.py:287
  91.3 0.2 copy.52
  91.5 0.2 reshape.125
  91.7 0.3 copy.48
  92.4 0.5 convolution_bitcast_fusion
  92.9 0.1 select_reduce_fusion.4
  93.0 0.2 copy.49
  93.3 0.7 add_divide_fusion
  (32 shorter events, 1.1 us)
Async XLA Ops:
  0.6 14.4 %copy-start = (bf16[256,2048]{1,0:T(8,128)(2,1)S(1)}, bf16[256,2048]{1,0:T(8,128)(2,1)}, u32[]{:S(2)}) copy-start(bf16[256,2048]{1,0:T(8,128)(2,1)} %param.13) | copy-start | bytes 3145732
  0.6 12.8 %copy-start.4 = (s32[256]{0:T(256)S(1)}, s32[256]{0:T(256)}, u32[]{:S(2)}) copy-start(s32[256]{0:T(256)} %param.14) | copy-start | bytes 3076
  2.5 24.7 %collective-permute-start.1 = (bf16[48,1536]{1,0:T(8,128)(2,1)}, bf16[48,1536]{1,0:T(8,128)(2,1)S(1)}, u32[]{:S(2)}, u32[]{:S(2)}) collective-permute-start(bf16[48,1536]{1,0:T(8,128)(2,1)} %get-tuple-element.11), channel_id=1, source_target_pairs={{1,0},{2,1},{3,2},{4,3},{5,4},{6,5},{7,6},{8,7},{9,8},{10,9},{11,1... | collective-permute-start | bytes 442376 | tf_op jit(solution)/shard_map/ppermute | solution.py:24
  3.8 23.4 %collective-permute-start = (bf16[48,1536]{1,0:T(8,128)(2,1)}, bf16[48,1536]{1,0:T(8,128)(2,1)S(1)}, u32[]{:S(2)}, u32[]{:S(2)}) collective-permute-start(bf16[48,1536]{1,0:T(8,128)(2,1)} %get-tuple-element.12), channel_id=1, source_target_pairs={{0,1},{1,2},{2,3},{3,4},{4,5},{5,6},{6,7},{7,8},{8,9},{9,10},{10,1... | collective-permute-start | bytes 442376 | tf_op jit(solution)/shard_map/ppermute | solution.py:24
  10.6 7.0 %copy-start.1 = (f32[1536,33]{0,1:T(8,128)S(1)}, f32[1536,33]{0,1:T(8,128)}, u32[]{:S(2)}) copy-start(f32[1536,33]{0,1:T(8,128)} %param.12) | copy-start | bytes 608260
  27.2 0.7 copy-start.2
  27.2 0.7 copy-start.3
  67.8 23.5 %all-to-all-start = ((bf16[16,144,128]{2,1,0:T(8,128)(2,1)}), bf16[16,144,128]{2,1,0:T(8,128)(2,1)S(1)}, u32[]{:S(2)}, u32[]{:S(2)}) async-start(bf16[16,144,128]{2,1,0:T(8,128)(2,1)} %bitcast.33), calls=%async_computation | async-start | bytes 1179648 | tf_op jit(solution)/shard_map/all_to_all | solution.py:287

commit v2 on v1

--- a/solution.py
+++ b/solution.py
@@ -13,7 +13,7 @@
 CAP = 8
 TILE = 256
 HALO = 48
-GROUP = 16
+GROUP = 64
 PACK = CAP * TW // 2 + 2 * CAP
 
 
@@ -50,11 +50,14 @@
     placed,
     sums,
     squares,
+    band_rows,
+    woven,
+    amp_cols,
 ):
     i = pl.program_id(0)
     last = pl.num_programs(0) - 1
     width = raw_ref.shape[1]
-    lanes = width // 128
+    tiles = width // NB - 1
     probes = width // CH_PROBE
     slots = placed.shape[0]
     rows = wide.shape[1] - TW
@@ -66,8 +69,10 @@
         spread = jnp.broadcast_to(taps_ref[...], (TILE, taps_ref.shape[1]))
         skewed = pltpu.roll(spread, 0, 1, stride=1, stride_axis=0)
         toep[...] = skewed.astype(jnp.bfloat16)
+        band_rows[...] = jnp.zeros_like(band_rows)
+        band_rows[:BAND, :] = whiten_ref[...]
         for p in range(probes):
-            part = whiten_ref[p * CH_PROBE : (p + 1) * CH_PROBE, :]
+            part = band_rows[:, p * CH_PROBE : (p + 1) * CH_PROBE].T
             part = jnp.concatenate([part, jnp.zeros((CH_PROBE, 384), jnp.float32)], axis=1)
             skewed = pltpu.roll(part, 512 - BAND // 2, 1, stride=1, stride_axis=0)
             mixer[p] = skewed[:, :CH_PROBE].T.astype(jnp.bfloat16)
@@ -87,8 +92,8 @@
         whole = jnp.concatenate(parts, axis=1).astype(jnp.float32)
         if scale is not None:
             whole = whole * scale
-        for c in range(lanes):
-            wide[c, pl.ds(start, size), :] = whole[:, c * 128 : (c + 1) * 128]
+        for c in range(tiles):
+            wide[c, pl.ds(start, size), :] = whole[:, c * NB : c * NB + 128]
 
     prev = jnp.where(i == 0, low_ref[HALO - 32 :, :], prev_ref[...])
     after = jnp.where(i == last, high_ref[:32, :], next_ref[...])
@@ -116,34 +121,37 @@
                 slot = four * 4 + j
                 k = used_s[slot]
                 r = rest_s[k]
-                rolled = pltpu.roll(temp_ref[k].astype(jnp.float32), lax.rem(r, 128), 1)
-                for half in range(2):
-                    at = lane + 128 * half - r
-                    placed[slot, half] = jnp.where((at >= 0) & (at < NB), rolled, 0.0)
-                    sums[slot, half] = jnp.zeros((TW, 128), jnp.float32)
+                pairs = temp_ref[k].astype(jnp.float32)
+                woven[j, pl.ds(0, TW // 2, stride=2), :] = pairs
+                woven[j, pl.ds(1, TW // 2, stride=2), :] = pltpu.roll(pairs, NB, 1)
+                rolled = pltpu.roll(woven[j], r, 1)
+                at = lane - r
+                placed[slot] = jnp.where((at >= 0) & (at < NB), rolled, 0.0)
+                sums[slot] = jnp.zeros((TW, 128), jnp.float32)
 
         squares[...] = jnp.zeros_like(squares)
 
-        @pl.loop(0, amp_ref.shape[0] // GROUP)
+        @pl.loop(0, amp_cols.shape[0] // GROUP)
         def _(group):
             first = pl.multiple_of(group * GROUP, GROUP)
             windows, places, folded = [], [], []
             for j in range(GROUP):
                 k = tmpl_s[first + j]
                 slot = slot_s[k]
-                window = wide[pl.ds(quot_s[k], 2), pl.ds(time_s[first + j], TW), :]
-                product = window * placed[slot]
-                total = product[0] + product[1]
-                folded.append(jnp.sum(total, axis=0, keepdims=True))
+                window = wide[quot_s[k], pl.ds(time_s[first + j], TW), :]
+                folded.append(jnp.sum(window * placed[slot], axis=0, keepdims=True))
                 windows.append(window)
                 places.append(slot)
             inner = jnp.sum(jnp.concatenate(folded, axis=0), axis=1, keepdims=True)
             amps = coef_ref[pl.ds(first, GROUP), :] * inner
-            amp_ref[pl.ds(first, GROUP), :] = amps
+            amp_cols[pl.ds(first, GROUP), :] = jnp.broadcast_to(amps, (GROUP, 128))
             for j in range(GROUP):
                 one = amps[j : j + 1, :]
-                sums[places[j]] += one[None] * windows[j]
+                sums[places[j]] += one * windows[j]
                 squares[pl.ds(places[j], 1), :] += jnp.broadcast_to(one * one, (1, 128))
+
+        for b in range(amp_ref.shape[0]):
+            amp_ref[b : b + 1, :] = amp_cols[b * 128 : (b + 1) * 128, :].T[:1, :]
 
         half_lane = lane[: TW // 2]
         aux_lane = lane[:CAP]
@@ -157,9 +165,7 @@
                 slot = owner * CAP + j
                 k = used_s[slot]
                 r = rest_s[k]
-                merged = jnp.where(lane >= r, sums[slot, 0], sums[slot, 1])
-                merged = jnp.where(r >= 128, sums[slot, 1], merged)
-                back = pltpu.roll(merged, lax.rem(256 - r, 128), 1)
+                back = pltpu.roll(sums[slot], lax.rem(128 - r, 128), 1)
                 lower = back[TW // 2 :]
                 both = jnp.where(half_lane < NB, back[: TW // 2], pltpu.roll(lower, NB, 1))
                 pack_ref[pl.ds(pl.multiple_of(start + j * 16, 16), 16), :] = both.astype(
@@ -198,10 +204,9 @@
 
     taps_b = taps.astype(jnp.bfloat16).astype(jnp.float32)
     taps_row = jnp.pad(taps_b, (2, 384 - 2 - taps.shape[0]))[None, :]
-    whiten_wide = jnp.pad(whiten, ((0, 0), (0, 128 - BAND)))
-    temp_wide = jnp.pad(templates.reshape(ntemp, TW, NB), ((0, 0), (0, 0), (0, 128 - NB)))
-    quot = jnp.minimum(template_base // 128, width // 128 - 2)
-    rest = template_base - quot * 128
+    temp_pairs = templates.reshape(ntemp, TW // 2, 2 * NB)
+    quot = jnp.minimum(template_base // NB, width // NB - 2)
+    rest = template_base - quot * NB
 
     tmpl = templates.astype(jnp.float32)
     energy_t = jnp.sum(tmpl * tmpl, axis=1)
@@ -239,27 +244,30 @@
                 pl.BlockSpec((HALO, width), fixed2),
                 pl.BlockSpec((HALO, width), fixed2),
                 pl.BlockSpec((1, 384), fixed2),
-                pl.BlockSpec((width, 128), fixed2),
-                pl.BlockSpec((ntemp, TW, 128), lambda i, *_: (0, 0, 0)),
+                pl.BlockSpec((BAND, width), fixed2),
+                pl.BlockSpec((ntemp, TW // 2, 128), lambda i, *_: (0, 0, 0)),
                 pl.BlockSpec((spikes, 1), fixed2),
             ],
             out_specs=[
                 pl.BlockSpec((TILE, width), lambda i, *_: (i, 0)),
-                pl.BlockSpec((spikes, 1), fixed2),
+                pl.BlockSpec((spikes // 128, 128), fixed2),
                 pl.BlockSpec((owners * PACK, 128), fixed2),
             ],
             scratch_shapes=[
-                pltpu.VMEM((width // 128, rows + TW, 128), jnp.float32),
+                pltpu.VMEM((width // NB - 1, rows + TW, 128), jnp.float32),
                 pltpu.VMEM((TILE, 384), jnp.bfloat16),
                 pltpu.VMEM((width // CH_PROBE, CH_PROBE, CH_PROBE), jnp.bfloat16),
-                pltpu.VMEM((slots, 2, TW, 128), jnp.float32),
-                pltpu.VMEM((slots, 2, TW, 128), jnp.float32),
+                pltpu.VMEM((slots, TW, 128), jnp.float32),
+                pltpu.VMEM((slots, TW, 128), jnp.float32),
                 pltpu.VMEM((slots, 128), jnp.float32),
+                pltpu.VMEM((128, width), jnp.float32),
+                pltpu.VMEM((4, TW, 128), jnp.float32),
+                pltpu.VMEM((spikes, 128), jnp.float32),
             ],
         ),
         out_shape=[
             jax.ShapeDtypeStruct((rows, width), jnp.bfloat16),
-            jax.ShapeDtypeStruct((spikes, 1), jnp.float32),
+            jax.ShapeDtypeStruct((spikes // 128, 128), jnp.float32),
             jax.ShapeDtypeStruct((owners * PACK, 128), jnp.bfloat16),
         ],
         compiler_params=pltpu.CompilerParams(
@@ -279,8 +287,8 @@
         low,
         high,
         taps_row,
-        whiten_wide,
-        temp_wide,
+        whiten.T,
+        temp_pairs,
         coef,
     )
 

time: 94.8 us -> 85.4 us (0.901)
  local copies, waits for them, and re-layouts: 15.7 us -> 7.14 us
  Pallas kernels: 39.9 us -> 37.6 us
  waiting for transfers between devices: 13.7 us -> 15.6 us
    reshape x1 -> x0, local copies, waits for them, and re-layouts: 3.91 us -> none  [shards(): templates.reshape(ntemp, TW, NB)]
    pad x2 -> x0, local copies, waits for them, and re-layouts: 3.86 us -> none  [the longest x1 2.1 us: shards(): whiten_wide = jnp.pad(whiten, ((0, 0), (0, 128 - BAND)))]
    pallas_call x1, Pallas kernels: 39.9 us -> 37.6 us  [shards(): pl.pallas_call(body, grid_spec=pltpu.PrefetchScalarGridSpec(num_scalar_pr...]
    all_to_all x1, waiting for transfers between devices: 13.7 us -> 15.5 us  [shards(): arrived = lax.all_to_all(packed.reshape(owners, PACK, 128), 'tm', 0, 0)]
    pallas_call x1 -> x0, other arithmetic: 1.85 us -> none  [shards(): pl.pallas_call(body, grid_spec=pltpu.PrefetchScalarGridSpec(num_scalar_pr...]
    unnamed x13 -> x6, local copies, waits for them, and re-layouts: 3.39 us -> 3.36 us
  transfers between devices with their start and end apart: 3 -> 3, of which waited for: 1 -> 1; matrix products, arithmetic and copies ran while one was open for 23% -> 15% of each run, Pallas kernels for 0% -> 0%
where the time goes in v2:
time: 85.4 us; the launch traced here: 84.6 us
  Pallas kernels  37.6 us (44%)
  waiting for transfers between devices  15.6 us (18%)
  starting transfers between devices  12.3 us (14%)
  other arithmetic  10.1 us (12%)
  local copies, waits for them, and re-layouts  7.14 us (8%)
  between operations  1.45 us (2%)
    pallas_call x1, Pallas kernels, shards(): pl.pallas_call(body, grid_spec=pltpu.PrefetchScalarGridSpec(num_scalar_pr...  37.6 us
    all_to_all x1, waiting for transfers between devices, shards(): arrived = lax.all_to_all(packed.reshape(owners, PACK, 128), 'tm', 0, 0)  15.5 us
    all_to_all x1, starting transfers between devices, shards(): arrived = lax.all_to_all(packed.reshape(owners, PACK, 128), 'tm', 0, 0)  7.94 us
    unnamed x6, local copies, waits for them, and re-layouts  3.36 us
    ppermute x1, starting transfers between devices, from_neighbours(): lax.ppermute(low_part, axis, forward)  3.04 us
  transfers between devices with their start and end apart: 3, of which 1 were waited for; matrix products, arithmetic and copies ran while one was open for 15% of the time, Pallas kernels for 0%

profile of v2, /device:TPU:0, one launch (start us, length us, event | category | flops | bytes accessed | tf_op | source)
XLA Modules:
  0.0 84.6 jit_solution(7825811453237962728)
XLA Ops:
  0.6 1.0 %fusion.8 = (bf16[48,1536]{1,0:T(8,128)(2,1)S(1)}, bf16[48,1536]{1,0:T(8,128)(2,1)S(1)}) fusion(bf16[2048,1536]{1,0:T(8,128)(2,1)} %next_ref.1), kind=kLoop, calls=%fused_computation.37 | loop fusion | bytes 589824 | tf_op jit(solution)/shard_map/slice | solution.py:202
  1.6 1.3 %collective-permute-start.1 = (bf16[48,1536]{1,0:T(8,128)(2,1)S(1)}, bf16[48,1536]{1,0:T(8,128)(2,1)S(1)}, u32[]{:S(2)}, u32[]{:S(2)}) collective-permute-start(bf16[48,1536]{1,0:T(8,128)(2,1)S(1)} %get-tuple-element.11), channel_id=1, source_target_pairs={{1,0},{2,1},{3,2},{4,3},{5,4},{6,5},{7,6},{8,7},{9,8},{10,9},{11,1... | collective-permute-start | bytes 442376 | tf_op jit(solution)/shard_map/ppermute | solution.py:24
  2.9 3.0 %collective-permute-start = (bf16[48,1536]{1,0:T(8,128)(2,1)S(1)}, bf16[48,1536]{1,0:T(8,128)(2,1)S(1)}, u32[]{:S(2)}, u32[]{:S(2)}) collective-permute-start(bf16[48,1536]{1,0:T(8,128)(2,1)S(1)} %get-tuple-element.12), channel_id=1, source_target_pairs={{0,1},{1,2},{2,3},{3,4},{4,5},{5,6},{6,7},{7,8},{8,9},{9,10},{10,1... | collective-permute-start | bytes 442376 | tf_op jit(solution)/shard_map/ppermute | solution.py:24
  6.7 0.9 %fusion = pred[256]{0:T(512)(128)(4,1)S(1)} fusion(s32[1024]{0:T(1024)} %tmpl_s.1), kind=kLoop, calls=%fused_computation.4 | loop fusion | flops 524032 | bytes 4352 | tf_op jit(solution)/shard_map/reduce_or | solution.py:215
  7.6 0.7 convert_element_type.37
  8.2 1.5 %multiply_reduce_fusion = f32[256]{0:T(256)S(1)} fusion(bf16[256,2048]{1,0:T(8,128)(2,1)} %param.13), kind=kLoop, calls=%fused_computation | loop fusion | flops 1572608 | bytes 1049600 | tf_op jit(solution)/shard_map/reduce_sum | solution.py:212
  9.7 0.1 broadcast_in_dim_reshape.2
  9.8 1.1 %select_reduce_fusion = f32[1024]{0:T(1024)S(1)} fusion(f32[256]{0:T(256)S(1)} %multiply_reduce_fusion, s32[1024]{0:T(1024)} %tmpl_s.1), kind=kLoop, calls=%fused_computation.2 | loop fusion | flops 785408 | bytes 9216 | tf_op jit(solution)/shard_map/reduce_sum | solution.py:214
  10.9 0.1 select_reduce_fusion.1
  11.0 0.3 select_reduce_fusion.2
  11.5 0.8 select_reduce_fusion.3
  12.3 0.2 copy.32
  12.6 1.3 %multiply_subtract_fusion = (s32[256]{0:T(256)}, s32[256]{0:T(256)}, s32[256]{0:T(256)}) fusion(s32[256]{0:T(256)} %param.14, pred[256]{0:T(512)(128)(4,1)S(1)} %fusion, s32[256]{0:T(256)S(1)} %add.67), kind=kLoop, calls=%fused_computation.31 | loop fusion | flops 4864 | bytes 5376 | tf_op jit(solution)/shard_map/sub | solution.py:209
  13.9 0.8 fusion.1.coef_ref
  14.8 0.6 reshape.127.taps_ref
  15.4 0.7 add.70.used_s
  16.1 2.5 %copy.40 = bf16[32,8,16,128]{3,2,1,0:T(8,128)(2,1)} copy(bf16[32,8,16,128]{3,1,2,0:T(8,128)(2,1)} %bitcast.33) | data formatting | bytes 2097152
  18.5 0.6 add_convert_fusion.edge_s
  19.1 0.6 copy-done
  19.9 37.6 %shard_map.121 = (bf16[2048,1536]{1,0:T(8,128)(2,1)}, f32[8,128]{1,0:T(8,128)}, bf16[2304,128]{1,0:T(8,128)(2,1)}) custom-call(s32[1024]{0:T(1024)} %time_s.1, s32[1024]{0:T(1024)} %tmpl_s.1, s32[256]{0:T(256)} %get-tuple-element.15.slot_s, s32[256]{0:T(256)} %get-tuple-element.10.quot_s, s32[256]{0:T(256)} %get-tuple-element.9.rest_s, s32[128]{0:T(128)} %add.70.used_s, ...), custom_call_target="tpu_custom_call" | custom-call | tf_op jit(solution)/shard_map/pallas_call | solution.py:235
  57.5 7.9 %all-to-all-start = ((bf16[16,144,128]{2,1,0:T(8,128)(2,1)}), bf16[16,144,128]{2,1,0:T(8,128)(2,1)S(1)}, u32[]{:S(2)}, u32[]{:S(2)}) async-start(bf16[16,144,128]{2,1,0:T(8,128)(2,1)} %bitcast.37), calls=%async_computation | async-start | bytes 1179648 | tf_op jit(solution)/shard_map/all_to_all | solution.py:295
  65.4 15.5 %all-to-all-done = bf16[16,144,128]{2,1,0:T(8,128)(2,1)S(1)} async-done(((bf16[16,144,128]{2,1,0:T(8,128)(2,1)}), bf16[16,144,128]{2,1,0:T(8,128)(2,1)S(1)}, u32[]{:S(2)}, u32[]{:S(2)}) %all-to-all-start) | async-done | bytes 589856 | tf_op jit(solution)/shard_map/all_to_all | solution.py:295
  81.0 0.2 copy.39
  81.2 0.2 reshape.125
  81.5 0.3 copy.35
  81.8 0.1 add.76
  82.0 0.1 convert_element_type.41
  82.1 0.5 convolution_bitcast_fusion
  82.6 0.1 select_reduce_fusion.4
  82.7 0.2 copy.36
  82.9 0.1 reshape.126
  83.0 1.6 %add_divide_fusion = f32[16,2048]{1,0:T(8,128)} fusion(f32[16,2048]{1,0:T(8,128)S(1)} %reshape.126, f32[16]{0:T(128)S(1)} %broadcast_add_fusion.2, bf16[256,2048]{1,0:T(8,128)(2,1)} %param.13, s32[]{:T(128)S(6)} %select_n.51), kind=kLoop, calls=%fused_computation.7 | loop fusion | flops 98304 | bytes 327748 | tf_op jit(solution)/shard_map/div | solution.py:307
  (21 shorter events, 0.6 us)
Async XLA Ops:
  1.6 17.5 %collective-permute-start.1 = (bf16[48,1536]{1,0:T(8,128)(2,1)S(1)}, bf16[48,1536]{1,0:T(8,128)(2,1)S(1)}, u32[]{:S(2)}, u32[]{:S(2)}) collective-permute-start(bf16[48,1536]{1,0:T(8,128)(2,1)S(1)} %get-tuple-element.11), channel_id=1, source_target_pairs={{1,0},{2,1},{3,2},{4,3},{5,4},{6,5},{7,6},{8,7},{9,8},{10,9},{11,1... | collective-permute-start | bytes 442376 | tf_op jit(solution)/shard_map/ppermute | solution.py:24
  2.9 16.2 %collective-permute-start = (bf16[48,1536]{1,0:T(8,128)(2,1)S(1)}, bf16[48,1536]{1,0:T(8,128)(2,1)S(1)}, u32[]{:S(2)}, u32[]{:S(2)}) collective-permute-start(bf16[48,1536]{1,0:T(8,128)(2,1)S(1)} %get-tuple-element.12), channel_id=1, source_target_pairs={{0,1},{1,2},{2,3},{3,4},{4,5},{5,6},{6,7},{7,8},{8,9},{9,10},{10,1... | collective-permute-start | bytes 442376 | tf_op jit(solution)/shard_map/ppermute | solution.py:24
  19.1 0.7 copy-start
  19.1 0.7 copy-start.1
  57.5 23.5 %all-to-all-start = ((bf16[16,144,128]{2,1,0:T(8,128)(2,1)}), bf16[16,144,128]{2,1,0:T(8,128)(2,1)S(1)}, u32[]{:S(2)}, u32[]{:S(2)}) async-start(bf16[16,144,128]{2,1,0:T(8,128)(2,1)} %bitcast.37), calls=%async_computation | async-start | bytes 1179648 | tf_op jit(solution)/shard_map/all_to_all | solution.py:295
